TPU v7x, 128 devices: a whole 4x4x4 slice. The times are simulated.
128 devices in a mesh: gx: 8 (over x, core), gy: 16 (over z, y).
Axes of the slice: x: 4, y: 4, z: 4, core: 2. Of those that a mesh axis runs over, the one named last changes fastest.
Arguments:
- rhs: bfloat16 [128, 262144], P(None, ('gx', 'gy')), may hold values from -6 to 6
- col_basis: bfloat16 [64, 262144], P(None, ('gx', 'gy')), may hold values from -0.375 to 0.375
- row_basis: bfloat16 [64, 262144], P(None, ('gx', 'gy')), may hold values from -0.75 to 0.75
- near_blocks: bfloat16 [4, 256, 262144], P(None, None, ('gx', 'gy')), may hold values from -0.1875 to 0.1875
- near_list: int32 [1024, 4], P(('gx', 'gy')), may hold values from 0 to 1023, as said below
- leaf_up: float32 [1024, 4096], P(('gx', 'gy')), may hold values from -0.5 to 0.5
- leaf_down: float32 [1024, 4096], P(('gx', 'gy')), may hold values from -0.75 to 0.75
- local_up: float32 [896, 4096], P(('gx', 'gy')), may hold values from -0.5 to 0.5
- local_down: float32 [896, 4096], P(('gx', 'gy')), may hold values from -0.75 to 0.75
- leaf_coupling: bfloat16 [1024, 64, 1024], P(('gx', 'gy')), may hold values from -0.1875 to 0.1875
- leaf_target: int32 [1024, 16], P(('gx', 'gy')), may hold values from 0 to 127, all different within a row; in each aligned block of 8 rows (0 to 7, 8 to 15, ...) at most 2 rows name the same one
- leaf_slot: int32 [1024, 16], P(('gx', 'gy')), may hold values from 0 to 7
- top_up: float32 [124, 4096], replicated, may hold values from -0.5 to 0.5
- top_down: float32 [124, 4096], replicated, may hold values from -0.75 to 0.75
- upper_coupling: bfloat16 [126, 4, 4096], replicated, may hold values from -0.375 to 0.375
- upper_partners: int32 [126, 4], replicated, may hold values from 0 to 63, as said below
Outputs:
- product: bfloat16 [128, 262144], P(None, ('gx', 'gy'))
Inputs may be any that keep to these rules, and one draw needn't show every extreme that they name: `near_list`: row t begins with t itself; its other entries are leaves at most 8 away from t, clipped to the range; in each aligned block of 8 rows some entry lies exactly 8 above its row and some exactly 8 below it before clipping. `leaf_target`: each row names 16 different devices; among the rows of one device no device is named more than 2 times, and some device is named exactly 2 times. `upper_partners`: row row(m, i) names only clusters of level m other than i, by their index within level m.
All inputs are finite; a program needn't handle non-finite values.
Results may differ from a plain program's by a relative error of at most 0.0058.
Values may be sent and summed in bfloat16 or wider, within the bound.
A program may use at most 192 MiB of HBM per device.

v0:
```python
import jax
import jax.numpy as jnp
from jax import lax
from jax.experimental import pallas as pl
from jax.experimental.pallas import tpu as pltpu
from jax.sharding import PartitionSpec as P

K = 64
R = 128
P_SIZE = 256
LEAF_DEV = 8
NEAR = 4
FAR_LEAF = 16
FAR_TOP = 4
NX = 8
NY = 16
D = NX * NY
HALF = K // 2
MESH = pl.DeviceIdType.MESH
BF = jnp.bfloat16
F32 = jnp.float32


def mm(a, b):
    return jnp.dot(a, b, preferred_element_type=F32)


def split(x):
    hi = x.astype(BF)
    return hi, (x - hi.astype(F32)).astype(BF)


def precise(a, w):
    a_hi, a_lo = split(a)
    w_hi, w_lo = split(w)
    return mm(a_hi, w_hi) + (mm(a_lo, w_hi) + mm(a_hi, w_lo))


def unroll(rows, count, squares, first):
    for q in range(K // 2):
        pair = rows[:, q * 2 * K:(q + 1) * 2 * K].astype(F32)
        for h in range(2):
            at = first * K + 2 * q + h
            squares[pl.ds(at, count, stride=K), :] = pair[:, h * K:(h + 1) * K]


def kernel(
    src_sm, near_sm, part_sm,
    rhs, col, leaf_up, leaf_down, local_up, local_down, code_a, code_b,
    row_hbm, near_hbm, coup_hbm, tup_hbm, tdn_hbm, ucp_hbm,
    out,
    rhs3, nearv, coupv, rowv, tupv, tdnv, ucpv,
    prods, send_a, recv_a, send_b, recv_b, meta_a, meta_b, codes_a, codes_b,
    send_a2, recv_a2, send_b2, recv_b2,
    roots, tiles_hi, tiles_lo, tops, squares, near_acc, tree_leaf,
    local_sem, send_sem, recv_sem,
):
    mx = lax.axis_index("gx")
    my = lax.axis_index("gy")
    me = mx * NY + my

    def fetch(src, dst, number):
        copy = pltpu.make_async_copy(src, dst, local_sem.at[number])
        copy.start()
        return copy

    def remote(src, dst, number, device):
        pltpu.make_async_remote_copy(
            src_ref=src, dst_ref=dst, send_sem=send_sem.at[number], recv_sem=recv_sem.at[number],
            device_id=device, device_id_type=MESH,
        ).start()

    def finish(ref, sem):
        pltpu.make_async_copy(ref, ref, sem).wait()

    def block(i):
        return squares[i * K:(i + 1) * K, :]

    def peers_x():
        return [lax.rem(mx + i, NX) for i in range(1, NX)]

    def peers_y():
        return [lax.rem(my + i, NY) for i in range(1, NY)]

    nxt = lax.rem(me + 1, D)
    prv = lax.rem(me + D - 1, D)
    sides = ((lax.div(nxt, NY), lax.rem(nxt, NY)), (lax.div(prv, NY), lax.rem(prv, NY)))

    barrier = pltpu.get_barrier_semaphore()
    for x in peers_x():
        pl.semaphore_signal(barrier, inc=1, device_id=(x, my), device_id_type=MESH)
    for y in peers_y():
        pl.semaphore_signal(barrier, inc=1, device_id=(mx, y), device_id_type=MESH)
    for side in sides:
        pl.semaphore_signal(barrier, inc=1, device_id=side, device_id_type=MESH)

    got_coup = fetch(coup_hbm, coupv, 0)
    got_near = fetch(near_hbm, nearv, 1)
    got_row = fetch(row_hbm, rowv, 2)
    got_tup = fetch(tup_hbm, tupv, 3)
    got_tdn = fetch(tdn_hbm, tdnv, 4)
    rows_up = [D - (D >> level - 1) + lax.div(me, 1 << level) for level in range(1, 7)]
    got_ucp = [fetch(ucp_hbm.at[rows_up[m]], ucpv.at[m], 5 + m) for m in range(6)]

    def part(ref, l):
        return ref[:, l * P_SIZE:(l + 1) * P_SIZE]

    nt = (((1,), (1,)), ((), ()))
    tn = (((0,), (0,)), ((), ()))
    low = [
        lax.dot_general(part(col, l), part(rhs, l), nt, preferred_element_type=F32).astype(BF)
        for l in range(LEAF_DEV)
    ]

    for l in range(LEAF_DEV):
        rhs3[LEAF_DEV + l] = part(rhs, l)
    own = rhs3.at[pl.ds(LEAF_DEV, LEAF_DEV)]
    pl.semaphore_wait(barrier, NX + NY)
    for j, side in enumerate(sides):
        remote(own, rhs3.at[pl.ds(2 * j * LEAF_DEV, LEAF_DEV)], j, side)
    for x in peers_x():
        remote(code_a.at[x], meta_a.at[mx], 2, (x, my))
    for y in peers_y():
        remote(code_b.at[y], meta_b.at[my], 3, (mx, y))
    meta_a[mx] = code_a[mx]
    meta_b[my] = code_b[my]

    got_coup.wait()
    for l in range(LEAF_DEV):
        product = lax.dot_general(coupv[l], low[l], tn, preferred_element_type=F32)
        prods[l * FAR_LEAF:(l + 1) * FAR_LEAF] = product.astype(BF).reshape(FAR_LEAF, K, R)

    def place_b(y):
        for x in range(NX):
            for c in range(2):
                product = prods[src_sm[(x * NY + y) * 2 + c]]
                send_b[y, x, c * HALF:(c + 1) * HALF, :] = product[HALF:]

    def step_b(i, _):
        y = lax.rem(my + i, NY)
        place_b(y)
        remote(send_b.at[y], recv_b.at[:, my], 4, (mx, y))
        return 0

    def place_a(x):
        for y in range(NY):
            for c in range(2):
                product = prods[src_sm[(x * NY + y) * 2 + c]]
                send_a[x, y, c * HALF:(c + 1) * HALF, :] = product[:HALF]

    def step_a(i, _):
        x = lax.rem(mx + i, NX)
        place_a(x)
        remote(send_a.at[x], recv_a.at[:, mx], 5, (x, my))
        return 0

    lax.fori_loop(1, NY, step_b, 0)
    lax.fori_loop(1, NX, step_a, 0)
    place_b(my)
    place_a(mx)
    recv_b[:, my] = send_b[my]
    recv_a[:, mx] = send_a[mx]

    coef = [
        lax.dot_general(part(rhs, l), part(col, l), nt, preferred_element_type=F32)
        for l in range(LEAF_DEV)
    ]
    unroll(leaf_up, 8, squares, 0)
    lifted = [precise(coef[l], block(l)) for l in range(LEAF_DEV)]
    unroll(local_up, 7, squares, 8)
    start = 8
    while len(lifted) > 1:
        coef = [lifted[2 * i] + lifted[2 * i + 1] for i in range(len(lifted) // 2)]
        lifted = [
            precise(coef[i], block(start + i)) for i in range(len(coef))
        ]
        start += len(coef)
    roots[my] = jnp.concatenate(split(lifted[0]), axis=1)
    for y in peers_y():
        remote(roots.at[my], roots.at[my], 6, (mx, y))

    got_near.wait()
    for l in range(LEAF_DEV):
        near_acc[:, l * P_SIZE:(l + 1) * P_SIZE] = mm(part(rhs, l), nearv[0, :, l * P_SIZE:(l + 1) * P_SIZE])

    finish(roots.at[pl.ds(0, NY - 1)], recv_sem.at[6])
    first_lanes = lax.broadcasted_iota(jnp.int32, (R, 2 * K), 1) < K
    for i in range(4):
        r = [roots[4 * i + h].astype(F32) for h in range(4)]
        r = [r[0] + r[1], r[2] + r[3]]
        r = [v + pltpu.roll(v, K, 1) for v in r]
        tiles_hi[mx * 4 + i] = jnp.where(first_lanes, r[0], r[1]).astype(BF)
    for x in peers_x():
        remote(tiles_hi.at[pl.ds(mx * 4, 4)], tiles_hi.at[pl.ds(mx * 4, 4)], 7, (x, my))

    for j in range(2):
        finish(own, recv_sem.at[j])
    for l in range(LEAF_DEV):
        total = near_acc[:, l * P_SIZE:(l + 1) * P_SIZE]
        for j in range(1, NEAR):
            source = rhs3[near_sm[l * NEAR + j]]
            total += mm(source, nearv[j, :, l * P_SIZE:(l + 1) * P_SIZE])
        near_acc[:, l * P_SIZE:(l + 1) * P_SIZE] = total

    got_tup.wait()

    def turn(g, _):
        unroll(tupv.at[pl.ds(g * 8, 8)], 8, tops, g * 8)
        return 0

    lax.fori_loop(0, 15, turn, 0)
    unroll(tupv.at[120:124], 4, tops, 120)
    unroll(local_down, 7, squares, 15)
    unroll(leaf_down, 8, squares, 22)
    got_tdn.wait()
    for m in range(5):
        unroll(tdnv.at[pl.ds(rows_up[m], 1)], 1, squares, 30 + m)
    for m in range(6):
        got_ucp[m].wait()
        unroll(ucpv.at[m], FAR_TOP, squares, 35 + m * FAR_TOP)

    finish(meta_a.at[pl.ds(0, NX - 1)], recv_sem.at[2])
    finish(meta_b.at[pl.ds(0, NY - 1)], recv_sem.at[3])
    lanes = lax.broadcasted_iota(jnp.int32, (NY, 128), 1) < 2 * HALF
    for q in range(NX // 2):
        codes_a[:, q * 128:(q + 1) * 128] = jnp.where(lanes, meta_a[2 * q], meta_a[2 * q + 1])
    lanes = lax.broadcasted_iota(jnp.int32, (NX, 128), 1) < 2 * HALF
    for q in range(NY // 2):
        codes_b[:, q * 128:(q + 1) * 128] = jnp.where(lanes, meta_b[2 * q], meta_b[2 * q + 1])

    def gathered(codes, recv, g):
        width = codes.shape[1]
        rows = lax.broadcasted_iota(jnp.int32, (LEAF_DEV * HALF, width), 0)
        hits = jnp.where(rows == codes[pl.ds(g, 1), :], 1.0, 0.0).astype(BF)
        return mm(hits, recv[g].reshape(width, R)).astype(BF)

    finish(recv_a.at[:, pl.ds(0, NX - 1)], recv_sem.at[5])

    def sum_a(i, _):
        y = lax.rem(my + i, NY)
        send_a2[y] = gathered(codes_a, recv_a, y)
        remote(send_a2.at[y], recv_a2.at[my], 8, (mx, y))
        return 0

    lax.fori_loop(1, NY, sum_a, 0)
    recv_a2[my] = gathered(codes_a, recv_a, my)
    finish(recv_b.at[:, pl.ds(0, NY - 1)], recv_sem.at[4])

    def sum_b(i, _):
        x = lax.rem(mx + i, NX)
        send_b2[x] = gathered(codes_b, recv_b, x)
        remote(send_b2.at[x], recv_b2.at[mx], 9, (x, my))
        return 0

    lax.fori_loop(1, NX, sum_b, 0)
    recv_b2[mx] = gathered(codes_b, recv_b, mx)

    finish(tiles_hi.at[pl.ds(0, 28)], recv_sem.at[7])

    def merge(t, _):
        halves = []
        for h in range(2):
            tile = 2 * t + h
            a = tiles_hi[tile]
            wh, wl = split(tops[pl.ds(tile * 2 * K, 2 * K), :])
            halves.append((a, wh, wl, tile))
        return halves

    def merge_first(t, _):
        merged = [mm(a, wh) + mm(a, wl) for a, wh, wl, _ in merge(t, None)]
        hi, lo = split(jnp.concatenate(merged, axis=1))
        tiles_hi[32 + t] = hi
        tiles_lo[t] = lo
        return 0

    def merge_next(t, _):
        merged = [
            mm(a, wh) + (mm(a, wl) + mm(tiles_lo[tile - 32], wh)) for a, wh, wl, tile in merge(t, None)
        ]
        hi, lo = split(jnp.concatenate(merged, axis=1))
        tiles_hi[32 + t] = hi
        tiles_lo[t] = lo
        return 0

    lax.fori_loop(0, 16, merge_first, 0)
    lax.fori_loop(16, 31, merge_next, 0)

    fars = []
    for m in range(6):
        total = None
        for j in range(FAR_TOP):
            partner = part_sm[rows_up[m] * FAR_TOP + j]
            tile = tiles_hi[64 - (64 >> m) + lax.div(partner, 2)].astype(F32)
            side = jnp.full((R, K), lax.rem(partner, 2), jnp.int32)
            picked = jnp.where(side == 0, tile[:, :K], tile[:, K:])
            term = mm(picked.astype(BF), block(35 + m * FAR_TOP + j).astype(BF))
            total = term if total is None else total + term
        fars.append(total)
    answer = fars[5]
    for m in range(4, -1, -1):
        answer = fars[m] + precise(answer, block(30 + m))
    answers = [precise(answer, block(15 + 6))]
    for count in (2, 4):
        start = 15 + LEAF_DEV - 2 * count
        answers = [precise(answers[i // 2], block(start + i)) for i in range(count)]
    for l in range(LEAF_DEV):
        tree_leaf[l] = precise(answers[l // 2], block(22 + l)).T

    got_row.wait()
    finish(recv_a2.at[pl.ds(0, NY - 1)], recv_sem.at[8])
    finish(recv_b2.at[pl.ds(0, NX - 1)], recv_sem.at[9])
    for l in range(LEAF_DEV):
        upper = recv_a2[0, l * HALF:(l + 1) * HALF, :].astype(F32)
        for s in range(1, NY):
            upper += recv_a2[s, l * HALF:(l + 1) * HALF, :].astype(F32)
        lower = recv_b2[0, l * HALF:(l + 1) * HALF, :].astype(F32)
        for s in range(1, NX):
            lower += recv_b2[s, l * HALF:(l + 1) * HALF, :].astype(F32)
        answer_low = (jnp.concatenate([upper, lower], axis=0) + tree_leaf[l]).astype(BF)
        far = lax.dot_general(answer_low, part(rowv, l), tn, preferred_element_type=F32)
        out[:, l * P_SIZE:(l + 1) * P_SIZE] = (far + part(near_acc, l)).astype(BF)

    for j in range(2):
        finish(own, send_sem.at[j])
    finish(meta_a.at[pl.ds(0, NX - 1)], send_sem.at[2])
    finish(meta_b.at[pl.ds(0, NY - 1)], send_sem.at[3])
    finish(send_b.at[pl.ds(0, NY - 1)], send_sem.at[4])
    finish(send_a.at[pl.ds(0, NX - 1)], send_sem.at[5])
    finish(roots.at[pl.ds(0, NY - 1)], send_sem.at[6])
    finish(tiles_hi.at[pl.ds(0, 28)], send_sem.at[7])
    finish(send_a2.at[pl.ds(0, NY - 1)], send_sem.at[8])
    finish(send_b2.at[pl.ds(0, NX - 1)], send_sem.at[9])


def body(
    rhs, col_basis, row_basis, near_blocks, near_list, leaf_up, leaf_down, local_up, local_down,
    leaf_coupling, leaf_target, leaf_slot, top_up, top_down, upper_coupling, upper_partners,
):
    total = LEAF_DEV * FAR_LEAF
    target = leaf_target.reshape(total)
    order = jnp.arange(total, dtype=jnp.int32)
    earlier = (target[:, None] == target[None, :]) & (order[None, :] < order[:, None])
    placed = 2 * target + jnp.sum(earlier.astype(jnp.int32), axis=1)
    matches = placed[None, :] == jnp.arange(2 * D, dtype=jnp.int32)[:, None]
    source = jnp.max(jnp.where(matches, order[None, :], 0), axis=1)
    slots = jnp.max(jnp.where(matches, leaf_slot.reshape(total)[None, :], -1), axis=1)
    slots = slots.reshape(NX, NY, 1, 2, 1)
    code = jnp.where(slots >= 0, slots * HALF + jnp.arange(HALF, dtype=jnp.int32), -1)
    code_a = jnp.broadcast_to(code, (NX, NY, 2, 2, HALF)).reshape(NX, NY, 4 * HALF)
    code_b = jnp.swapaxes(code_a, 0, 1)
    device = lax.axis_index("gx") * NY + lax.axis_index("gy")
    near = near_list.reshape(-1) - (device * LEAF_DEV - LEAF_DEV)
    smem = pl.BlockSpec(memory_space=pltpu.SMEM)
    vmem = pl.BlockSpec(memory_space=pltpu.VMEM)
    hbm = pl.BlockSpec(memory_space=pl.ANY)
    width = LEAF_DEV * P_SIZE
    return pl.pallas_call(
        kernel,
        out_shape=jax.ShapeDtypeStruct((R, width), BF),
        in_specs=[smem] * 3 + [vmem] * 8 + [hbm] * 6,
        out_specs=vmem,
        scratch_shapes=[
            pltpu.VMEM((3 * LEAF_DEV, R, P_SIZE), BF),
            pltpu.VMEM((NEAR, P_SIZE, width), BF),
            pltpu.VMEM((LEAF_DEV, K, FAR_LEAF * K), BF),
            pltpu.VMEM((K, width), BF),
            pltpu.VMEM((D - 4, K * K), F32),
            pltpu.VMEM((D - 4, K * K), F32),
            pltpu.VMEM((6, FAR_TOP, K * K), BF),
            pltpu.VMEM((total, K, R), BF),
            pltpu.VMEM((NX, NY, K, R), BF),
            pltpu.VMEM((NY, NX, K, R), BF),
            pltpu.VMEM((NY, NX, K, R), BF),
            pltpu.VMEM((NX, NY, K, R), BF),
            pltpu.VMEM((NX, NY, 128), jnp.int32),
            pltpu.VMEM((NY, NX, 128), jnp.int32),
            pltpu.VMEM((NY, NX * K), jnp.int32),
            pltpu.VMEM((NX, NY * K), jnp.int32),
            pltpu.VMEM((NY, LEAF_DEV * HALF, R), BF),
            pltpu.VMEM((NY, LEAF_DEV * HALF, R), BF),
            pltpu.VMEM((NX, LEAF_DEV * HALF, R), BF),
            pltpu.VMEM((NX, LEAF_DEV * HALF, R), BF),
            pltpu.VMEM((NY, R, 2 * K), BF),
            pltpu.VMEM((63, R, 2 * K), BF),
            pltpu.VMEM((31, R, 2 * K), BF),
            pltpu.VMEM(((D - 4) * K, K), F32),
            pltpu.VMEM((59 * K, K), F32),
            pltpu.VMEM((R, width), F32),
            pltpu.VMEM((LEAF_DEV, K, R), F32),
            pltpu.SemaphoreType.DMA((11,)),
            pltpu.SemaphoreType.DMA((10,)),
            pltpu.SemaphoreType.DMA((10,)),
        ],
        compiler_params=pltpu.CompilerParams(
            collective_id=0, has_side_effects=True, vmem_limit_bytes=60 * 1024 * 1024
        ),
    )(
        source, near, upper_partners.reshape(-1),
        rhs, col_basis, leaf_up, leaf_down, local_up, local_down, code_a, code_b,
        row_basis, near_blocks, leaf_coupling, top_up, top_down, upper_coupling,
    )


def solution(mesh):
    flat = ("gx", "gy")
    placed = (
        P(None, flat), P(None, flat), P(None, flat), P(None, None, flat),
        P(flat, None), P(flat, None), P(flat, None), P(flat, None), P(flat, None),
        P(flat, None, None), P(flat, None), P(flat, None),
        P(), P(), P(), P(),
    )
    return jax.shard_map(body, mesh=mesh, in_specs=placed, out_specs=P(None, flat), check_vma=False)
```

profile of v0, /device:TPU:5, one launch (start us, length us, event | category | flops | bytes accessed | tf_op | source)
XLA Modules:
  0.0 93.2 jit_solution(14769176306324925231)
XLA Ops:
  0.0 0.8 reshape.53
  0.8 0.2 convert_reduce_fusion
  1.0 0.8 broadcast_in_dim.47
  1.7 0.7 select_reduce_fusion
  2.5 0.7 broadcast_subtract_fusion
  3.2 0.1 copy.24
  3.2 0.7 sub.14.near_sm
  3.9 0.2 ge.16
  4.1 0.1 mul.36
  4.2 0.3 add_select_fusion
  4.6 0.8 copy.25
  5.4 0.7 reshape.54.part_sm
  6.1 0.1 broadcast_in_dim.52
  6.2 0.2 reshape.55
  6.4 0.0 copy-start
  6.4 0.7 copy.28.code_a
  7.1 0.0 copy-done
  7.1 84.2 %shard_map.154 = bf16[128,2048]{1,0:T(8,128)(2,1)} custom-call(s32[256]{0:T(256)} %get-tuple-element.6.src_sm, s32[32]{0:T(128)} %sub.14.near_sm, s32[504]{0:T(512)} %reshape.54.part_sm, bf16[128,2048]{1,0:T(8,128)(2,1)} %rhs.1, bf16[64,2048]{1,0:T(8,128)(2,1)} %col.1, f32[8,4096]{1,0:T(8,128)} %leaf_up.1, f32[8,4096]{1,0:T(8,128)} %leaf_down.1, ...), custom_call_target="tpu_custom_call" | custom-call | tf_op jit(solution)/shard_map/pallas_call | solution.py:357
  91.3 1.9 %copy.30 = bf16[128,2048]{1,0:T(8,128)(2,1)} copy(bf16[128,2048]{1,0:T(8,128)(2,1)} %shard_map.154) | data formatting | bytes 1048576
  (5 shorter events, 0.1 us)
Async XLA Ops:
  6.4 0.7 copy-start
where the time goes:
time: 93.5 us; the launch traced here: 93.2 us
  Pallas kernels  84.2 us (90%)
  local copies, waits for them, and re-layouts  6.94 us (7%)
  other arithmetic  1.94 us (2%)
    pallas_call x1, Pallas kernels, body(): pl.pallas_call(kernel, out_shape=jax.ShapeDtypeStruct((R, width), BF), in...  84.2 us
    unnamed x4, local copies, waits for them, and re-layouts  2.69 us

commit v1 on v0

v1 whole, which is shorter than its diff:
```python
import jax
import jax.numpy as jnp
from jax import lax
from jax.experimental import pallas as pl
from jax.experimental.pallas import tpu as pltpu
from jax.sharding import PartitionSpec as P

K = 64
R = 128
P_SIZE = 256
LEAF_DEV = 8
NEAR = 4
FAR_LEAF = 16
FAR_TOP = 4
NX = 8
NY = 16
D = NX * NY
HALF = K // 2
MESH = pl.DeviceIdType.MESH
BF = jnp.bfloat16
F32 = jnp.float32


def mm(a, b):
    return jnp.dot(a, b, preferred_element_type=F32)


def split(x):
    hi = x.astype(BF)
    return hi, (x - hi.astype(F32)).astype(BF)


def precise(a, w):
    a_hi, a_lo = split(a)
    w_hi, w_lo = split(w)
    return mm(a_hi, w_hi) + (mm(a_lo, w_hi) + mm(a_hi, w_lo))


def unroll(rows, count, squares, first):
    for q in range(K // 2):
        pair = rows[:, q * 2 * K:(q + 1) * 2 * K].astype(F32)
        for h in range(2):
            at = first * K + 2 * q + h
            squares[pl.ds(at, count, stride=K), :] = pair[:, h * K:(h + 1) * K]


def kernel(
    near_sm, part_sm,
    rhs, col, leaf_up, leaf_down, local_up, local_down, target, slot,
    row_hbm, near_hbm, coup_hbm, tup_hbm, tdn_hbm, ucp_hbm,
    out,
    rhs3, nearv, coupv, rowv, tupv, tdnv, ucpv,
    table, table_sm, code, code_b,
    prods, send_a, recv_a, send_b, recv_b, meta_a, meta_b, codes_a, codes_b,
    send_a2, recv_a2, send_b2, recv_b2, send_a3, recv_a3, send_b3, recv_b3,
    roots, tiles_hi, tiles_lo, tops, squares, near_acc, tree_leaf,
    local_sem, send_sem, recv_sem,
):
    mx = lax.axis_index("gx")
    my = lax.axis_index("gy")
    me = mx * NY + my
    cx, cc = lax.div(mx, 2), lax.rem(mx, 2)
    cz, cy = lax.div(my, 4), lax.rem(my, 4)
    zc = cz * 2 + cc

    def at_x(x):
        return (x * 2 + cc, my)

    def at_y(y):
        return (mx, cz * 4 + y)

    def at_z(z):
        return (mx, z * 4 + cy)

    def at_gx(x):
        return (x, my)

    def at_zc(g):
        return (cx * 2 + lax.rem(g, 2), lax.div(g, 2) * 4 + cy)

    sibling = (cx * 2 + 1 - cc, my)

    def fetch(src, dst, number):
        copy = pltpu.make_async_copy(src, dst, local_sem.at[number])
        copy.start()
        return copy

    def remote(src, dst, number, device):
        pltpu.make_async_remote_copy(
            src_ref=src, dst_ref=dst, send_sem=send_sem.at[number], recv_sem=recv_sem.at[number],
            device_id=device, device_id_type=MESH,
        ).start()

    def finish(ref, sem):
        pltpu.make_async_copy(ref, ref, sem).wait()

    def block(i):
        return squares[i * K:(i + 1) * K, :]

    def others(mine, count):
        return [lax.rem(mine + i, count) for i in range(1, count)]

    nxt = lax.rem(me + 1, D)
    prv = lax.rem(me + D - 1, D)
    sides = ((lax.div(nxt, NY), lax.rem(nxt, NY)), (lax.div(prv, NY), lax.rem(prv, NY)))

    barrier = pltpu.get_barrier_semaphore()
    peers = [at_gx(x) for x in others(mx, NX)] + [at_zc(g) for g in others(zc, 8)]
    peers += [at_y(y) for y in others(cy, 4)] + list(sides)
    for peer in peers:
        pl.semaphore_signal(barrier, inc=1, device_id=peer, device_id_type=MESH)

    got_coup = fetch(coup_hbm, coupv, 0)
    got_near = fetch(near_hbm, nearv, 1)
    got_row = fetch(row_hbm, rowv, 2)
    got_tup = fetch(tup_hbm, tupv, 3)
    got_tdn = fetch(tdn_hbm, tdnv, 4)
    rows_up = [D - (D >> level - 1) + lax.div(me, 1 << level) for level in range(1, 7)]
    got_ucp = [fetch(ucp_hbm.at[rows_up[m]], ucpv.at[m], 5 + m) for m in range(6)]

    lane = lax.broadcasted_iota(jnp.int32, (LEAF_DEV, D), 1)
    row = lax.broadcasted_iota(jnp.int32, (LEAF_DEV, D), 0)
    named = jnp.full((LEAF_DEV, D), -1, jnp.int32)
    for j in range(FAR_LEAF):
        entry = (row * FAR_LEAF + j) * LEAF_DEV + slot[:, j:j + 1]
        named = jnp.where(target[:, j:j + 1] == lane, entry, named)
    last = jnp.max(named, axis=0, keepdims=True)
    first = jnp.min(jnp.where(named < 0, 1 << 20, named), axis=0, keepdims=True)
    first = jnp.where(last < 0, -1, first)
    last = jnp.where(last == first, -1, last)
    lists = jnp.where(row == 0, first, last)
    table[...] = lax.shift_right_logical(jnp.maximum(lists, 0), 3)
    got_table = fetch(table, table_sm, 11)

    def part(ref, l):
        return ref[:, l * P_SIZE:(l + 1) * P_SIZE]

    nt = (((1,), (1,)), ((), ()))
    tn = (((0,), (0,)), ((), ()))
    low = [
        lax.dot_general(part(col, l), part(rhs, l), nt, preferred_element_type=F32).astype(BF)
        for l in range(LEAF_DEV)
    ]
    for l in range(LEAF_DEV):
        rhs3[LEAF_DEV + l] = part(rhs, l)
    own = rhs3.at[pl.ds(LEAF_DEV, LEAF_DEV)]
    wide = lax.broadcasted_iota(jnp.int32, (D, D), 1)
    pick = jnp.where(
        (wide & HALF) == 0,
        jnp.broadcast_to(first, (D, D)).T,
        jnp.broadcast_to(last, (D, D)).T,
    )
    code[...] = jnp.where(pick < 0, -1, (pick & (LEAF_DEV - 1)) * HALF + (wide & (HALF - 1)))
    for g in range(8):
        for y in range(4):
            base = (g % 2) * NY + (g // 2) * 4 + y
            code_b[g, y * 4:(y + 1) * 4, :] = code[pl.ds(base, 4, stride=2 * NY), :]

    pl.semaphore_wait(barrier, len(peers))
    for j, side in enumerate(sides):
        remote(own, rhs3.at[pl.ds(2 * j * LEAF_DEV, LEAF_DEV)], j, side)
    for x in others(mx, NX):
        remote(code.at[pl.ds(pl.multiple_of(x * NY, NY), NY)], meta_a.at[mx], 2, at_gx(x))
    for g in others(zc, 8):
        remote(code_b.at[g], meta_b.at[zc], 3, at_zc(g))
    meta_a[mx] = code[pl.ds(pl.multiple_of(mx * NY, NY), NY), :]
    meta_b[zc] = code_b[zc]

    got_coup.wait()
    for l in range(LEAF_DEV):
        product = lax.dot_general(coupv[l], low[l], tn, preferred_element_type=F32)
        prods[l * FAR_LEAF:(l + 1) * FAR_LEAF] = product.astype(BF).reshape(FAR_LEAF, K, R)

    got_table.wait()

    def place_a(x):
        for g in range(NY):
            for c in range(2):
                product = prods[table_sm[c, x * NY + g]]
                send_a[x, g, c * HALF:(c + 1) * HALF, :] = product[:HALF]

    def place_b(g):
        for y in range(4):
            for x in range(4):
                device = (x * 2 + lax.rem(g, 2)) * NY + lax.div(g, 2) * 4 + y
                for c in range(2):
                    product = prods[table_sm[c, device]]
                    send_b[g, y * 4 + x, c * HALF:(c + 1) * HALF, :] = product[HALF:]

    def step_first(i, _):
        x = lax.rem(mx + i, NX)
        place_a(x)
        remote(send_a.at[x], recv_a.at[:, mx], 5, at_gx(x))
        g = lax.rem(zc + i, 8)
        place_b(g)
        remote(send_b.at[g], recv_b.at[:, zc], 4, at_zc(g))
        return 0

    lax.fori_loop(1, NX, step_first, 0)
    place_a(mx)
    place_b(zc)
    recv_a[:, mx] = send_a[mx]
    recv_b[:, zc] = send_b[zc]

    coef = [
        lax.dot_general(part(rhs, l), part(col, l), nt, preferred_element_type=F32)
        for l in range(LEAF_DEV)
    ]
    unroll(leaf_up, 8, squares, 0)
    lifted = [precise(coef[l], block(l)) for l in range(LEAF_DEV)]
    unroll(local_up, 7, squares, 8)
    start = 8
    while len(lifted) > 1:
        coef = [lifted[2 * i] + lifted[2 * i + 1] for i in range(len(lifted) // 2)]
        lifted = [precise(coef[i], block(start + i)) for i in range(len(coef))]
        start += len(coef)
    roots[cy] = jnp.concatenate(split(lifted[0]), axis=1)
    for y in others(cy, 4):
        remote(roots.at[cy], roots.at[cy], 6, at_y(y))

    got_near.wait()
    for l in range(LEAF_DEV):
        near_acc[:, l * P_SIZE:(l + 1) * P_SIZE] = mm(part(rhs, l), nearv[0, :, l * P_SIZE:(l + 1) * P_SIZE])

    finish(roots.at[pl.ds(0, 3)], recv_sem.at[6])
    first_lanes = lax.broadcasted_iota(jnp.int32, (R, 2 * K), 1) < K
    r = [roots[h].astype(F32) for h in range(4)]
    r = [r[0] + r[1], r[2] + r[3]]
    r = [v + pltpu.roll(v, K, 1) for v in r]
    mine = tiles_hi.at[mx * 4 + cz]
    mine[...] = jnp.where(first_lanes, r[0], r[1]).astype(BF)
    for z in others(cz, 4):
        remote(mine, mine, 7, at_z(z))

    for j in range(2):
        finish(own, recv_sem.at[j])
    for l in range(LEAF_DEV):
        total = near_acc[:, l * P_SIZE:(l + 1) * P_SIZE]
        for j in range(1, NEAR):
            at = near_sm[l, j] - (me * LEAF_DEV - LEAF_DEV)
            source = rhs3[jnp.minimum(jnp.maximum(at, 0), 3 * LEAF_DEV - 1)]
            total += mm(source, nearv[j, :, l * P_SIZE:(l + 1) * P_SIZE])
        near_acc[:, l * P_SIZE:(l + 1) * P_SIZE] = total

    got_tup.wait()

    def turn(g, _):
        unroll(tupv.at[pl.ds(g * 8, 8)], 8, tops, g * 8)
        return 0

    lax.fori_loop(0, 15, turn, 0)
    unroll(tupv.at[120:124], 4, tops, 120)
    unroll(local_down, 7, squares, 15)
    unroll(leaf_down, 8, squares, 22)
    got_tdn.wait()
    for m in range(5):
        unroll(tdnv.at[pl.ds(rows_up[m], 1)], 1, squares, 30 + m)
    for m in range(6):
        got_ucp[m].wait()
        unroll(ucpv.at[m], FAR_TOP, squares, 35 + m * FAR_TOP)

    finish(tiles_hi.at[pl.ds(0, 3)], recv_sem.at[7])
    plane = tiles_hi.at[pl.ds(mx * 4, 4)]
    for x in others(cx, 4):
        remote(plane, plane, 10, at_x(x))

    finish(meta_a.at[pl.ds(0, 7)], recv_sem.at[2])
    finish(meta_b.at[pl.ds(0, 7)], recv_sem.at[3])
    lanes = lax.broadcasted_iota(jnp.int32, (NY, 128), 1) < 2 * HALF
    for q in range(NX // 2):
        codes_a[:, q * 128:(q + 1) * 128] = jnp.where(lanes, meta_a[2 * q], meta_a[2 * q + 1])
        codes_b[:, q * 128:(q + 1) * 128] = jnp.where(lanes, meta_b[2 * q], meta_b[2 * q + 1])

    def gathered(codes, recv, g):
        width = codes.shape[1]
        rows = lax.broadcasted_iota(jnp.int32, (LEAF_DEV * HALF, width), 0)
        hits = jnp.where(rows == codes[pl.ds(g, 1), :], 1.0, 0.0).astype(BF)
        return mm(hits, recv[g].reshape(width, R)).astype(BF)

    finish(recv_a.at[:, pl.ds(0, 7)], recv_sem.at[5])

    def sum_a(i, _):
        z = lax.rem(cz + i, 4)
        for y in range(4):
            send_a2[z, y] = gathered(codes_a, recv_a, z * 4 + y)
        remote(send_a2.at[z], recv_a2.at[cz], 8, at_z(z))
        return 0

    lax.fori_loop(1, 4, sum_a, 0)
    for y in range(4):
        recv_a2[cz, y] = gathered(codes_a, recv_a, cz * 4 + y)
    finish(recv_b.at[:, pl.ds(0, 7)], recv_sem.at[4])

    def sum_b(i, _):
        y = lax.rem(cy + i, 4)
        for x in range(4):
            send_b2[y, x] = gathered(codes_b, recv_b, y * 4 + x)
        remote(send_b2.at[y], recv_b2.at[cy], 9, at_y(y))
        return 0

    lax.fori_loop(1, 4, sum_b, 0)
    for x in range(4):
        recv_b2[cy, x] = gathered(codes_b, recv_b, cy * 4 + x)

    finish(tiles_hi.at[pl.ds(0, 12)], recv_sem.at[10])
    for x in range(4):
        half = tiles_hi.at[pl.ds((x * 2 + cc) * 4, 4)]
        remote(half, half, 11, sibling)

    finish(tiles_hi.at[pl.ds(0, 16)], recv_sem.at[11])

    def merge(t):
        halves = []
        for h in range(2):
            tile = 2 * t + h
            wh, wl = split(tops[pl.ds(tile * 2 * K, 2 * K), :])
            halves.append((tiles_hi[tile], wh, wl, tile))
        return halves

    def keep(t, merged):
        hi, lo = split(jnp.concatenate(merged, axis=1))
        tiles_hi[32 + t] = hi
        tiles_lo[t] = lo
        return 0

    def merge_first(t, _):
        return keep(t, [mm(a, wh) + mm(a, wl) for a, wh, wl, _ in merge(t)])

    def merge_next(t, _):
        return keep(t, [
            mm(a, wh) + (mm(a, wl) + mm(tiles_lo[tile - 32], wh)) for a, wh, wl, tile in merge(t)
        ])

    for t in range(31):
        if t < 16:
            merge_first(t, 0)
        else:
            merge_next(t, 0)

    def summed(recv, place):
        total = recv[0, place].astype(F32)
        for s in range(1, 4):
            total += recv[s, place].astype(F32)
        return total.astype(BF)

    finish(recv_a2.at[pl.ds(0, 3)], recv_sem.at[8])
    for y in others(cy, 4):
        send_a3[y] = summed(recv_a2, y)
        remote(send_a3.at[y], recv_a3.at[cy], 12, at_y(y))
    recv_a3[cy] = summed(recv_a2, cy)
    finish(recv_b2.at[pl.ds(0, 3)], recv_sem.at[9])
    for x in others(cx, 4):
        send_b3[x] = summed(recv_b2, x)
        remote(send_b3.at[x], recv_b3.at[cx], 13, at_x(x))
    recv_b3[cx] = summed(recv_b2, cx)

    fars = []
    for m in range(6):
        total = None
        for j in range(FAR_TOP):
            partner = part_sm[rows_up[m], j]
            tile = tiles_hi[64 - (64 >> m) + lax.div(partner, 2)].astype(F32)
            side = jnp.full((R, K), lax.rem(partner, 2), jnp.int32)
            picked = jnp.where(side == 0, tile[:, :K], tile[:, K:])
            term = mm(picked.astype(BF), block(35 + m * FAR_TOP + j).astype(BF))
            total = term if total is None else total + term
        fars.append(total)
    answer = fars[5]
    for m in range(4, -1, -1):
        answer = fars[m] + precise(answer, block(30 + m))
    answers = [precise(answer, block(15 + 6))]
    for count in (2, 4):
        start = 15 + LEAF_DEV - 2 * count
        answers = [precise(answers[i // 2], block(start + i)) for i in range(count)]
    for l in range(LEAF_DEV):
        tree_leaf[l] = precise(answers[l // 2], block(22 + l)).T

    got_row.wait()
    finish(recv_a3.at[pl.ds(0, 3)], recv_sem.at[12])
    finish(recv_b3.at[pl.ds(0, 3)], recv_sem.at[13])
    for l in range(LEAF_DEV):
        rows = slice(l * HALF, (l + 1) * HALF)
        upper = recv_a3[0, rows, :].astype(F32)
        lower = recv_b3[0, rows, :].astype(F32)
        for s in range(1, 4):
            upper += recv_a3[s, rows, :].astype(F32)
            lower += recv_b3[s, rows, :].astype(F32)
        answer_low = (jnp.concatenate([upper, lower], axis=0) + tree_leaf[l]).astype(BF)
        far = lax.dot_general(answer_low, part(rowv, l), tn, preferred_element_type=F32)
        out[:, l * P_SIZE:(l + 1) * P_SIZE] = (far + part(near_acc, l)).astype(BF)

    for j in range(2):
        finish(own, send_sem.at[j])
    finish(meta_a.at[pl.ds(0, 7)], send_sem.at[2])
    finish(meta_b.at[pl.ds(0, 7)], send_sem.at[3])
    finish(send_b.at[pl.ds(0, 7)], send_sem.at[4])
    finish(send_a.at[pl.ds(0, 7)], send_sem.at[5])
    finish(roots.at[pl.ds(0, 3)], send_sem.at[6])
    finish(tiles_hi.at[pl.ds(0, 3)], send_sem.at[7])
    finish(send_a2.at[pl.ds(0, 3)], send_sem.at[8])
    finish(send_b2.at[pl.ds(0, 3)], send_sem.at[9])
    finish(tiles_hi.at[pl.ds(0, 12)], send_sem.at[10])
    finish(tiles_hi.at[pl.ds(0, 16)], send_sem.at[11])
    finish(send_a3.at[pl.ds(0, 3)], send_sem.at[12])
    finish(send_b3.at[pl.ds(0, 3)], send_sem.at[13])


def body(
    rhs, col_basis, row_basis, near_blocks, near_list, leaf_up, leaf_down, local_up, local_down,
    leaf_coupling, leaf_target, leaf_slot, top_up, top_down, upper_coupling, upper_partners,
):
    smem = pl.BlockSpec(memory_space=pltpu.SMEM)
    vmem = pl.BlockSpec(memory_space=pltpu.VMEM)
    hbm = pl.BlockSpec(memory_space=pl.ANY)
    width = LEAF_DEV * P_SIZE
    leaf_rows = LEAF_DEV * HALF
    return pl.pallas_call(
        kernel,
        out_shape=jax.ShapeDtypeStruct((R, width), BF),
        in_specs=[smem] * 2 + [vmem] * 8 + [hbm] * 6,
        out_specs=vmem,
        scratch_shapes=[
            pltpu.VMEM((3 * LEAF_DEV, R, P_SIZE), BF),
            pltpu.VMEM((NEAR, P_SIZE, width), BF),
            pltpu.VMEM((LEAF_DEV, K, FAR_LEAF * K), BF),
            pltpu.VMEM((K, width), BF),
            pltpu.VMEM((D - 4, K * K), F32),
            pltpu.VMEM((D - 4, K * K), F32),
            pltpu.VMEM((6, FAR_TOP, K * K), BF),
            pltpu.VMEM((8, D), jnp.int32),
            pltpu.SMEM((8, D), jnp.int32),
            pltpu.VMEM((D, D), jnp.int32),
            pltpu.VMEM((8, NY, D), jnp.int32),
            pltpu.VMEM((LEAF_DEV * FAR_LEAF, K, R), BF),
            pltpu.VMEM((8, NY, K, R), BF),
            pltpu.VMEM((NY, 8, K, R), BF),
            pltpu.VMEM((8, NY, K, R), BF),
            pltpu.VMEM((NY, 8, K, R), BF),
            pltpu.VMEM((8, NY, D), jnp.int32),
            pltpu.VMEM((8, NY, D), jnp.int32),
            pltpu.VMEM((NY, 8 * K), jnp.int32),
            pltpu.VMEM((NY, 8 * K), jnp.int32),
            pltpu.VMEM((4, 4, leaf_rows, R), BF),
            pltpu.VMEM((4, 4, leaf_rows, R), BF),
            pltpu.VMEM((4, 4, leaf_rows, R), BF),
            pltpu.VMEM((4, 4, leaf_rows, R), BF),
            pltpu.VMEM((4, leaf_rows, R), BF),
            pltpu.VMEM((4, leaf_rows, R), BF),
            pltpu.VMEM((4, leaf_rows, R), BF),
            pltpu.VMEM((4, leaf_rows, R), BF),
            pltpu.VMEM((4, R, 2 * K), BF),
            pltpu.VMEM((63, R, 2 * K), BF),
            pltpu.VMEM((31, R, 2 * K), BF),
            pltpu.VMEM(((D - 4) * K, K), F32),
            pltpu.VMEM((59 * K, K), F32),
            pltpu.VMEM((R, width), F32),
            pltpu.VMEM((LEAF_DEV, K, R), F32),
            pltpu.SemaphoreType.DMA((12,)),
            pltpu.SemaphoreType.DMA((14,)),
            pltpu.SemaphoreType.DMA((14,)),
        ],
        compiler_params=pltpu.CompilerParams(
            collective_id=0, has_side_effects=True, vmem_limit_bytes=60 * 1024 * 1024
        ),
    )(
        near_list, upper_partners,
        rhs, col_basis, leaf_up, leaf_down, local_up, local_down, leaf_target, leaf_slot,
        row_basis, near_blocks, leaf_coupling, top_up, top_down, upper_coupling,
    )


def solution(mesh):
    flat = ("gx", "gy")
    placed = (
        P(None, flat), P(None, flat), P(None, flat), P(None, None, flat),
        P(flat, None), P(flat, None), P(flat, None), P(flat, None), P(flat, None),
        P(flat, None, None), P(flat, None), P(flat, None),
        P(), P(), P(), P(),
    )
    return jax.shard_map(body, mesh=mesh, in_specs=placed, out_specs=P(None, flat), check_vma=False)
```

time: 93.5 us -> 74.6 us (0.80)
  the two profiles are of different devices: /device:TPU:5 before, /device:TPU:16 now
where the time goes in v1:
time: 74.6 us; the launch traced here: 74.3 us
  Pallas kernels  69.7 us (93%)
  local copies, waits for them, and re-layouts  4.65 us (6%)
    pallas_call x1, Pallas kernels, body(): pl.pallas_call(kernel, out_shape=jax.ShapeDtypeStruct((R, width), BF), in...  69.7 us
    unnamed x3, local copies, waits for them, and re-layouts  4.65 us

profile of v1, /device:TPU:16, one launch (start us, length us, event | category | flops | bytes accessed | tf_op | source)
XLA Modules:
  0.0 74.3 jit_solution(10262815566058740067)
XLA Ops:
  0.0 1.3 %copy.17.near_sm = s32[8,4]{1,0:T(8,128)} copy(s32[8,4]{0,1:T(4,128)} %param.20) | data formatting | bytes 256 | tf_op args[4]
  1.3 1.4 %copy.18.part_sm = s32[126,4]{1,0:T(8,128)} copy(s32[126,4]{0,1:T(4,128)} %param.31) | data formatting | bytes 4032 | tf_op args[15]
  2.8 69.7 %shard_map.154 = bf16[128,2048]{1,0:T(8,128)(2,1)} custom-call(s32[8,4]{1,0:T(8,128)} %copy.17.near_sm, s32[126,4]{1,0:T(8,128)} %copy.18.part_sm, bf16[128,2048]{1,0:T(8,128)(2,1)} %rhs.1, bf16[64,2048]{1,0:T(8,128)(2,1)} %col.1, f32[8,4096]{1,0:T(8,128)} %leaf_up.1, f32[8,4096]{1,0:T(8,128)} %leaf_down.1, f32[7,4096]{1,0:T(8,128)} %local_up.1, ...), custom_call_target="tpu_custom_call" | custom-call | tf_op jit(solution)/shard_map/pallas_call | solution.py:417
  72.4 1.9 %copy.20 = bf16[128,2048]{1,0:T(8,128)(2,1)} copy(bf16[128,2048]{1,0:T(8,128)(2,1)} %shard_map.154) | data formatting | bytes 1048576

commit v2 on v1

--- a/solution.py
+++ b/solution.py
@@ -49,7 +49,7 @@
     rhs, col, leaf_up, leaf_down, local_up, local_down, target, slot,
     row_hbm, near_hbm, coup_hbm, tup_hbm, tdn_hbm, ucp_hbm,
     out,
-    rhs3, nearv, coupv, rowv, tupv, tdnv, ucpv,
+    rhs3, wrapped, nearv, coupv, rowv, tupv, tdnv, ucpv,
     table, table_sm, code, code_b,
     prods, send_a, recv_a, send_b, recv_b, meta_a, meta_b, codes_a, codes_b,
     send_a2, recv_a2, send_b2, recv_b2, send_a3, recv_a3, send_b3, recv_b3,
@@ -100,13 +100,14 @@
     def others(mine, count):
         return [lax.rem(mine + i, count) for i in range(1, count)]
 
-    nxt = lax.rem(me + 1, D)
-    prv = lax.rem(me + D - 1, D)
-    sides = ((lax.div(nxt, NY), lax.rem(nxt, NY)), (lax.div(prv, NY), lax.rem(prv, NY)))
+    above = lax.rem(me + 4, D)
+    below = lax.rem(me + D - 4, D)
+    above = (lax.div(above, NY), lax.rem(above, NY))
+    below = (lax.div(below, NY), lax.rem(below, NY))
 
     barrier = pltpu.get_barrier_semaphore()
     peers = [at_gx(x) for x in others(mx, NX)] + [at_zc(g) for g in others(zc, 8)]
-    peers += [at_y(y) for y in others(cy, 4)] + list(sides)
+    peers += [at_y(y) for y in others(cy, 4)] + [above, below]
     for peer in peers:
         pl.semaphore_signal(barrier, inc=1, device_id=peer, device_id_type=MESH)
 
@@ -152,26 +153,44 @@
     )
     code[...] = jnp.where(pick < 0, -1, (pick & (LEAF_DEV - 1)) * HALF + (wide & (HALF - 1)))
     for g in range(8):
-        for y in range(4):
-            base = (g % 2) * NY + (g // 2) * 4 + y
-            code_b[g, y * 4:(y + 1) * 4, :] = code[pl.ds(base, 4, stride=2 * NY), :]
-
+        for x in range(4):
+            base = (x * 2 + g % 2) * NY + (g // 2) * 4
+            code_b[g, x * 4:(x + 1) * 4, :] = code[base:base + 4, :]
+
+    meta_a[mx] = code[pl.ds(pl.multiple_of(mx * NY, NY), NY), :]
+    meta_b[zc] = code_b[zc]
+
+    got_coup.wait()
+    for l in range(LEAF_DEV):
+        product = lax.dot_general(coupv[l], low[l], tn, preferred_element_type=F32)
+        prods[l * FAR_LEAF:(l + 1) * FAR_LEAF] = product.astype(BF).reshape(FAR_LEAF, K, R)
+
+    got_table.wait()
     pl.semaphore_wait(barrier, len(peers))
-    for j, side in enumerate(sides):
-        remote(own, rhs3.at[pl.ds(2 * j * LEAF_DEV, LEAF_DEV)], j, side)
+    before = rhs3.at[pl.ds(0, LEAF_DEV)]
+    after = rhs3.at[pl.ds(2 * LEAF_DEV, LEAF_DEV)]
+    up, down = at_y(lax.rem(cy + 1, 4)), at_y(lax.rem(cy + 3, 4))
+    starts, ends = cy == 0, cy == 3
+
+    @pl.when(ends)
+    def _():
+        remote(own, wrapped, 15, up)
+        remote(own, after, 1, down)
+
+    @pl.when(starts)
+    def _():
+        remote(own, before, 0, up)
+        remote(own, wrapped, 15, down)
+
+    @pl.when(jnp.logical_and(cy > 0, cy < 3))
+    def _():
+        remote(own, before, 0, up)
+        remote(own, after, 1, down)
+
     for x in others(mx, NX):
         remote(code.at[pl.ds(pl.multiple_of(x * NY, NY), NY)], meta_a.at[mx], 2, at_gx(x))
     for g in others(zc, 8):
         remote(code_b.at[g], meta_b.at[zc], 3, at_zc(g))
-    meta_a[mx] = code[pl.ds(pl.multiple_of(mx * NY, NY), NY), :]
-    meta_b[zc] = code_b[zc]
-
-    got_coup.wait()
-    for l in range(LEAF_DEV):
-        product = lax.dot_general(coupv[l], low[l], tn, preferred_element_type=F32)
-        prods[l * FAR_LEAF:(l + 1) * FAR_LEAF] = product.astype(BF).reshape(FAR_LEAF, K, R)
-
-    got_table.wait()
 
     def place_a(x):
         for g in range(NY):
@@ -180,12 +199,12 @@
                 send_a[x, g, c * HALF:(c + 1) * HALF, :] = product[:HALF]
 
     def place_b(g):
-        for y in range(4):
-            for x in range(4):
+        for x in range(4):
+            for y in range(4):
                 device = (x * 2 + lax.rem(g, 2)) * NY + lax.div(g, 2) * 4 + y
                 for c in range(2):
                     product = prods[table_sm[c, device]]
-                    send_b[g, y * 4 + x, c * HALF:(c + 1) * HALF, :] = product[HALF:]
+                    send_b[g, x * 4 + y, c * HALF:(c + 1) * HALF, :] = product[HALF:]
 
     def step_first(i, _):
         x = lax.rem(mx + i, NX)
@@ -232,16 +251,6 @@
     for z in others(cz, 4):
         remote(mine, mine, 7, at_z(z))
 
-    for j in range(2):
-        finish(own, recv_sem.at[j])
-    for l in range(LEAF_DEV):
-        total = near_acc[:, l * P_SIZE:(l + 1) * P_SIZE]
-        for j in range(1, NEAR):
-            at = near_sm[l, j] - (me * LEAF_DEV - LEAF_DEV)
-            source = rhs3[jnp.minimum(jnp.maximum(at, 0), 3 * LEAF_DEV - 1)]
-            total += mm(source, nearv[j, :, l * P_SIZE:(l + 1) * P_SIZE])
-        near_acc[:, l * P_SIZE:(l + 1) * P_SIZE] = total
-
     got_tup.wait()
 
     def turn(g, _):
@@ -260,10 +269,15 @@
         unroll(ucpv.at[m], FAR_TOP, squares, 35 + m * FAR_TOP)
 
     finish(tiles_hi.at[pl.ds(0, 3)], recv_sem.at[7])
-    plane = tiles_hi.at[pl.ds(mx * 4, 4)]
+    column = tiles_hi.at[mx * 4 + cy]
     for x in others(cx, 4):
-        remote(plane, plane, 10, at_x(x))
-
+        remote(column, column, 10, at_x(x))
+
+    finish(tiles_hi.at[pl.ds(0, 3)], recv_sem.at[10])
+    for x in others(cx, 4):
+        column = tiles_hi.at[(x * 2 + cc) * 4 + cy]
+        for y in others(cy, 4):
+            remote(column, column, 14, at_y(y))
     finish(meta_a.at[pl.ds(0, 7)], recv_sem.at[2])
     finish(meta_b.at[pl.ds(0, 7)], recv_sem.at[3])
     lanes = lax.broadcasted_iota(jnp.int32, (NY, 128), 1) < 2 * HALF
@@ -280,29 +294,40 @@
     finish(recv_a.at[:, pl.ds(0, 7)], recv_sem.at[5])
 
     def sum_a(i, _):
-        z = lax.rem(cz + i, 4)
+        y = lax.rem(cy + i, 4)
+        for z in range(4):
+            send_a2[y, z] = gathered(codes_a, recv_a, z * 4 + y)
+        remote(send_a2.at[y], recv_a2.at[cy], 8, at_y(y))
+        return 0
+
+    lax.fori_loop(1, 4, sum_a, 0)
+    for z in range(4):
+        recv_a2[cy, z] = gathered(codes_a, recv_a, z * 4 + cy)
+    finish(recv_b.at[:, pl.ds(0, 7)], recv_sem.at[4])
+
+    @pl.when(starts)
+    def _():
+        finish(own, recv_sem.at[15])
+        remote(wrapped, before, 16, above)
+
+    @pl.when(ends)
+    def _():
+        finish(own, recv_sem.at[15])
+        remote(wrapped, after, 16, below)
+
+
+    def sum_b(i, _):
+        x = lax.rem(cx + i, 4)
         for y in range(4):
-            send_a2[z, y] = gathered(codes_a, recv_a, z * 4 + y)
-        remote(send_a2.at[z], recv_a2.at[cz], 8, at_z(z))
+            send_b2[x, y] = gathered(codes_b, recv_b, x * 4 + y)
+        remote(send_b2.at[x], recv_b2.at[cx], 9, at_x(x))
         return 0
 
-    lax.fori_loop(1, 4, sum_a, 0)
+    lax.fori_loop(1, 4, sum_b, 0)
     for y in range(4):
-        recv_a2[cz, y] = gathered(codes_a, recv_a, cz * 4 + y)
-    finish(recv_b.at[:, pl.ds(0, 7)], recv_sem.at[4])
-
-    def sum_b(i, _):
-        y = lax.rem(cy + i, 4)
-        for x in range(4):
-            send_b2[y, x] = gathered(codes_b, recv_b, y * 4 + x)
-        remote(send_b2.at[y], recv_b2.at[cy], 9, at_y(y))
-        return 0
-
-    lax.fori_loop(1, 4, sum_b, 0)
-    for x in range(4):
-        recv_b2[cy, x] = gathered(codes_b, recv_b, cy * 4 + x)
-
-    finish(tiles_hi.at[pl.ds(0, 12)], recv_sem.at[10])
+        recv_b2[cx, y] = gathered(codes_b, recv_b, cx * 4 + y)
+
+    finish(tiles_hi.at[pl.ds(0, 9)], recv_sem.at[14])
     for x in range(4):
         half = tiles_hi.at[pl.ds((x * 2 + cc) * 4, 4)]
         remote(half, half, 11, sibling)
@@ -344,21 +369,21 @@
         return total.astype(BF)
 
     finish(recv_a2.at[pl.ds(0, 3)], recv_sem.at[8])
+    for z in others(cz, 4):
+        send_a3[z] = summed(recv_a2, z)
+        remote(send_a3.at[z], recv_a3.at[cz], 12, at_z(z))
+    recv_a3[cz] = summed(recv_a2, cz)
+    finish(recv_b2.at[pl.ds(0, 3)], recv_sem.at[9])
     for y in others(cy, 4):
-        send_a3[y] = summed(recv_a2, y)
-        remote(send_a3.at[y], recv_a3.at[cy], 12, at_y(y))
-    recv_a3[cy] = summed(recv_a2, cy)
-    finish(recv_b2.at[pl.ds(0, 3)], recv_sem.at[9])
-    for x in others(cx, 4):
-        send_b3[x] = summed(recv_b2, x)
-        remote(send_b3.at[x], recv_b3.at[cx], 13, at_x(x))
-    recv_b3[cx] = summed(recv_b2, cx)
+        send_b3[y] = summed(recv_b2, y)
+        remote(send_b3.at[y], recv_b3.at[cy], 13, at_y(y))
+    recv_b3[cy] = summed(recv_b2, cy)
 
     fars = []
     for m in range(6):
         total = None
         for j in range(FAR_TOP):
-            partner = part_sm[rows_up[m], j]
+            partner = part_sm[j, rows_up[m]]
             tile = tiles_hi[64 - (64 >> m) + lax.div(partner, 2)].astype(F32)
             side = jnp.full((R, K), lax.rem(partner, 2), jnp.int32)
             picked = jnp.where(side == 0, tile[:, :K], tile[:, K:])
@@ -375,6 +400,26 @@
     for l in range(LEAF_DEV):
         tree_leaf[l] = precise(answers[l // 2], block(22 + l)).T
 
+    @pl.when(cy > 0)
+    def _():
+        finish(own, recv_sem.at[0])
+
+    @pl.when(cy < 3)
+    def _():
+        finish(own, recv_sem.at[1])
+
+    @pl.when(jnp.logical_or(starts, ends))
+    def _():
+        finish(own, recv_sem.at[16])
+
+    for l in range(LEAF_DEV):
+        total = near_acc[:, l * P_SIZE:(l + 1) * P_SIZE]
+        for j in range(1, NEAR):
+            at = near_sm[j, l] - (me * LEAF_DEV - LEAF_DEV)
+            source = rhs3[jnp.minimum(jnp.maximum(at, 0), 3 * LEAF_DEV - 1)]
+            total += mm(source, nearv[j, :, l * P_SIZE:(l + 1) * P_SIZE])
+        near_acc[:, l * P_SIZE:(l + 1) * P_SIZE] = total
+
     got_row.wait()
     finish(recv_a3.at[pl.ds(0, 3)], recv_sem.at[12])
     finish(recv_b3.at[pl.ds(0, 3)], recv_sem.at[13])
@@ -389,8 +434,19 @@
         far = lax.dot_general(answer_low, part(rowv, l), tn, preferred_element_type=F32)
         out[:, l * P_SIZE:(l + 1) * P_SIZE] = (far + part(near_acc, l)).astype(BF)
 
-    for j in range(2):
-        finish(own, send_sem.at[j])
+    @pl.when(cy < 3)
+    def _():
+        finish(own, send_sem.at[0])
+
+    @pl.when(cy > 0)
+    def _():
+        finish(own, send_sem.at[1])
+
+    @pl.when(jnp.logical_or(starts, ends))
+    def _():
+        finish(own, send_sem.at[15])
+        finish(own, send_sem.at[16])
+
     finish(meta_a.at[pl.ds(0, 7)], send_sem.at[2])
     finish(meta_b.at[pl.ds(0, 7)], send_sem.at[3])
     finish(send_b.at[pl.ds(0, 7)], send_sem.at[4])
@@ -399,7 +455,8 @@
     finish(tiles_hi.at[pl.ds(0, 3)], send_sem.at[7])
     finish(send_a2.at[pl.ds(0, 3)], send_sem.at[8])
     finish(send_b2.at[pl.ds(0, 3)], send_sem.at[9])
-    finish(tiles_hi.at[pl.ds(0, 12)], send_sem.at[10])
+    finish(tiles_hi.at[pl.ds(0, 3)], send_sem.at[10])
+    finish(tiles_hi.at[pl.ds(0, 9)], send_sem.at[14])
     finish(tiles_hi.at[pl.ds(0, 16)], send_sem.at[11])
     finish(send_a3.at[pl.ds(0, 3)], send_sem.at[12])
     finish(send_b3.at[pl.ds(0, 3)], send_sem.at[13])
@@ -421,6 +478,7 @@
         out_specs=vmem,
         scratch_shapes=[
             pltpu.VMEM((3 * LEAF_DEV, R, P_SIZE), BF),
+            pltpu.VMEM((LEAF_DEV, R, P_SIZE), BF),
             pltpu.VMEM((NEAR, P_SIZE, width), BF),
             pltpu.VMEM((LEAF_DEV, K, FAR_LEAF * K), BF),
             pltpu.VMEM((K, width), BF),
@@ -456,14 +514,14 @@
             pltpu.VMEM((R, width), F32),
             pltpu.VMEM((LEAF_DEV, K, R), F32),
             pltpu.SemaphoreType.DMA((12,)),
-            pltpu.SemaphoreType.DMA((14,)),
-            pltpu.SemaphoreType.DMA((14,)),
+            pltpu.SemaphoreType.DMA((17,)),
+            pltpu.SemaphoreType.DMA((17,)),
         ],
         compiler_params=pltpu.CompilerParams(
             collective_id=0, has_side_effects=True, vmem_limit_bytes=60 * 1024 * 1024
         ),
     )(
-        near_list, upper_partners,
+        near_list.T, upper_partners.T,
         rhs, col_basis, leaf_up, leaf_down, local_up, local_down, leaf_target, leaf_slot,
         row_basis, near_blocks, leaf_coupling, top_up, top_down, upper_coupling,
     )

time: 74.6 us -> 67.4 us (0.903)
  the two profiles are of different devices: /device:TPU:16 before, /device:TPU:6 now
where the time goes in v2:
time: 67.4 us; the launch traced here: 66.9 us
  Pallas kernels  65 us (96%)
  local copies, waits for them, and re-layouts  1.88 us (3%)
    pallas_call x1, Pallas kernels, body(): pl.pallas_call(kernel, out_shape=jax.ShapeDtypeStruct((R, width), BF), in...  65 us
    unnamed x1, local copies, waits for them, and re-layouts  1.88 us

profile of v2, /device:TPU:6, one launch (start us, length us, event | category | flops | bytes accessed | tf_op | source)
XLA Modules:
  0.0 66.9 jit_solution(18271180332920000122)
XLA Ops:
  0.0 65.0 %shard_map.154 = bf16[128,2048]{1,0:T(8,128)(2,1)} custom-call(s32[4,8]{1,0:T(4,128)} %bitcast.2, s32[4,126]{1,0:T(4,128)} %bitcast.3, bf16[128,2048]{1,0:T(8,128)(2,1)} %rhs.1, bf16[64,2048]{1,0:T(8,128)(2,1)} %col.1, f32[8,4096]{1,0:T(8,128)} %leaf_up.1, f32[8,4096]{1,0:T(8,128)} %leaf_down.1, f32[7,4096]{1,0:T(8,128)} %local_up.1, f32[7,4096]{1,0:T(8,128)} %local_down.1, ...), custom_call_target="tpu_custom_call" | custom-call | tf_op jit(solution)/shard_map/pallas_call | solution.py:474
  65.0 1.9 %copy.18 = bf16[128,2048]{1,0:T(8,128)(2,1)} copy(bf16[128,2048]{1,0:T(8,128)(2,1)} %shard_map.154) | data formatting | bytes 1048576

commit v3 on v2

--- a/solution.py
+++ b/solution.py
@@ -166,61 +166,6 @@
         prods[l * FAR_LEAF:(l + 1) * FAR_LEAF] = product.astype(BF).reshape(FAR_LEAF, K, R)
 
     got_table.wait()
-    pl.semaphore_wait(barrier, len(peers))
-    before = rhs3.at[pl.ds(0, LEAF_DEV)]
-    after = rhs3.at[pl.ds(2 * LEAF_DEV, LEAF_DEV)]
-    up, down = at_y(lax.rem(cy + 1, 4)), at_y(lax.rem(cy + 3, 4))
-    starts, ends = cy == 0, cy == 3
-
-    @pl.when(ends)
-    def _():
-        remote(own, wrapped, 15, up)
-        remote(own, after, 1, down)
-
-    @pl.when(starts)
-    def _():
-        remote(own, before, 0, up)
-        remote(own, wrapped, 15, down)
-
-    @pl.when(jnp.logical_and(cy > 0, cy < 3))
-    def _():
-        remote(own, before, 0, up)
-        remote(own, after, 1, down)
-
-    for x in others(mx, NX):
-        remote(code.at[pl.ds(pl.multiple_of(x * NY, NY), NY)], meta_a.at[mx], 2, at_gx(x))
-    for g in others(zc, 8):
-        remote(code_b.at[g], meta_b.at[zc], 3, at_zc(g))
-
-    def place_a(x):
-        for g in range(NY):
-            for c in range(2):
-                product = prods[table_sm[c, x * NY + g]]
-                send_a[x, g, c * HALF:(c + 1) * HALF, :] = product[:HALF]
-
-    def place_b(g):
-        for x in range(4):
-            for y in range(4):
-                device = (x * 2 + lax.rem(g, 2)) * NY + lax.div(g, 2) * 4 + y
-                for c in range(2):
-                    product = prods[table_sm[c, device]]
-                    send_b[g, x * 4 + y, c * HALF:(c + 1) * HALF, :] = product[HALF:]
-
-    def step_first(i, _):
-        x = lax.rem(mx + i, NX)
-        place_a(x)
-        remote(send_a.at[x], recv_a.at[:, mx], 5, at_gx(x))
-        g = lax.rem(zc + i, 8)
-        place_b(g)
-        remote(send_b.at[g], recv_b.at[:, zc], 4, at_zc(g))
-        return 0
-
-    lax.fori_loop(1, NX, step_first, 0)
-    place_a(mx)
-    place_b(zc)
-    recv_a[:, mx] = send_a[mx]
-    recv_b[:, zc] = send_b[zc]
-
     coef = [
         lax.dot_general(part(rhs, l), part(col, l), nt, preferred_element_type=F32)
         for l in range(LEAF_DEV)
@@ -233,14 +178,60 @@
         coef = [lifted[2 * i] + lifted[2 * i + 1] for i in range(len(lifted) // 2)]
         lifted = [precise(coef[i], block(start + i)) for i in range(len(coef))]
         start += len(coef)
+    pl.semaphore_wait(barrier, len(peers))
     roots[cy] = jnp.concatenate(split(lifted[0]), axis=1)
     for y in others(cy, 4):
         remote(roots.at[cy], roots.at[cy], 6, at_y(y))
 
-    got_near.wait()
-    for l in range(LEAF_DEV):
-        near_acc[:, l * P_SIZE:(l + 1) * P_SIZE] = mm(part(rhs, l), nearv[0, :, l * P_SIZE:(l + 1) * P_SIZE])
-
+    before = rhs3.at[pl.ds(0, LEAF_DEV)]
+    after = rhs3.at[pl.ds(2 * LEAF_DEV, LEAF_DEV)]
+    up, down = at_y(lax.rem(cy + 1, 4)), at_y(lax.rem(cy + 3, 4))
+    starts, ends = cy == 0, cy == 3
+
+    @pl.when(ends)
+    def _():
+        remote(own, wrapped, 15, up)
+        remote(own, after, 1, down)
+
+    @pl.when(starts)
+    def _():
+        remote(own, before, 0, up)
+        remote(own, wrapped, 15, down)
+
+    @pl.when(jnp.logical_and(cy > 0, cy < 3))
+    def _():
+        remote(own, before, 0, up)
+        remote(own, after, 1, down)
+
+    for x in others(mx, NX):
+        remote(code.at[pl.ds(pl.multiple_of(x * NY, NY), NY)], meta_a.at[mx], 2, at_gx(x))
+    for g in others(zc, 8):
+        remote(code_b.at[g], meta_b.at[zc], 3, at_zc(g))
+
+    def place_a(x):
+        for g in range(NY):
+            for c in range(2):
+                product = prods[table_sm[c, x * NY + g]]
+                send_a[x, g, c * HALF:(c + 1) * HALF, :] = product[:HALF]
+
+    def place_b(g):
+        for x in range(4):
+            for y in range(4):
+                device = (x * 2 + lax.rem(g, 2)) * NY + lax.div(g, 2) * 4 + y
+                for c in range(2):
+                    product = prods[table_sm[c, device]]
+                    send_b[g, x * 4 + y, c * HALF:(c + 1) * HALF, :] = product[HALF:]
+
+    def step_first(i, _):
+        x = lax.rem(mx + i, NX)
+        place_a(x)
+        remote(send_a.at[x], recv_a.at[:, mx], 5, at_gx(x))
+        g = lax.rem(zc + i, 8)
+        place_b(g)
+        remote(send_b.at[g], recv_b.at[:, zc], 4, at_zc(g))
+        return 0
+
+    lax.fori_loop(1, 3, step_first, 0)
     finish(roots.at[pl.ds(0, 3)], recv_sem.at[6])
     first_lanes = lax.broadcasted_iota(jnp.int32, (R, 2 * K), 1) < K
     r = [roots[h].astype(F32) for h in range(4)]
@@ -250,6 +241,28 @@
     mine[...] = jnp.where(first_lanes, r[0], r[1]).astype(BF)
     for z in others(cz, 4):
         remote(mine, mine, 7, at_z(z))
+
+    lax.fori_loop(3, 5, step_first, 0)
+    finish(tiles_hi.at[pl.ds(0, 3)], recv_sem.at[7])
+    column = tiles_hi.at[mx * 4 + cy]
+    for x in others(cx, 4):
+        remote(column, column, 10, at_x(x))
+
+    lax.fori_loop(5, 7, step_first, 0)
+    finish(tiles_hi.at[pl.ds(0, 3)], recv_sem.at[10])
+    for x in others(cx, 4):
+        column = tiles_hi.at[(x * 2 + cc) * 4 + cy]
+        for y in others(cy, 4):
+            remote(column, column, 14, at_y(y))
+    lax.fori_loop(7, 8, step_first, 0)
+    place_a(mx)
+    place_b(zc)
+    recv_a[:, mx] = send_a[mx]
+    recv_b[:, zc] = send_b[zc]
+
+    got_near.wait()
+    for l in range(LEAF_DEV):
+        near_acc[:, l * P_SIZE:(l + 1) * P_SIZE] = mm(part(rhs, l), nearv[0, :, l * P_SIZE:(l + 1) * P_SIZE])
 
     got_tup.wait()
 
@@ -268,16 +281,17 @@
         got_ucp[m].wait()
         unroll(ucpv.at[m], FAR_TOP, squares, 35 + m * FAR_TOP)
 
-    finish(tiles_hi.at[pl.ds(0, 3)], recv_sem.at[7])
-    column = tiles_hi.at[mx * 4 + cy]
-    for x in others(cx, 4):
-        remote(column, column, 10, at_x(x))
-
-    finish(tiles_hi.at[pl.ds(0, 3)], recv_sem.at[10])
-    for x in others(cx, 4):
-        column = tiles_hi.at[(x * 2 + cc) * 4 + cy]
-        for y in others(cy, 4):
-            remote(column, column, 14, at_y(y))
+    @pl.when(starts)
+    def _():
+        finish(own, recv_sem.at[15])
+        remote(wrapped, before, 16, above)
+
+    @pl.when(ends)
+    def _():
+        finish(own, recv_sem.at[15])
+        remote(wrapped, after, 16, below)
+
+
     finish(meta_a.at[pl.ds(0, 7)], recv_sem.at[2])
     finish(meta_b.at[pl.ds(0, 7)], recv_sem.at[3])
     lanes = lax.broadcasted_iota(jnp.int32, (NY, 128), 1) < 2 * HALF
@@ -304,17 +318,6 @@
     for z in range(4):
         recv_a2[cy, z] = gathered(codes_a, recv_a, z * 4 + cy)
     finish(recv_b.at[:, pl.ds(0, 7)], recv_sem.at[4])
-
-    @pl.when(starts)
-    def _():
-        finish(own, recv_sem.at[15])
-        remote(wrapped, before, 16, above)
-
-    @pl.when(ends)
-    def _():
-        finish(own, recv_sem.at[15])
-        remote(wrapped, after, 16, below)
-
 
     def sum_b(i, _):
         x = lax.rem(cx + i, 4)

time: 67.4 us -> 65.1 us (0.966)
  Pallas kernels: 65 us -> 63 us
    pallas_call x1, Pallas kernels: 65 us -> 63 us  [body(): pl.pallas_call(kernel, out_shape=jax.ShapeDtypeStruct((R, width), BF), in...]
where the time goes in v3:
time: 65.1 us; the launch traced here: 64.9 us
  Pallas kernels  63 us (97%)
  local copies, waits for them, and re-layouts  1.88 us (3%)
    pallas_call x1, Pallas kernels, body(): pl.pallas_call(kernel, out_shape=jax.ShapeDtypeStruct((R, width), BF), in...  63 us
    unnamed x1, local copies, waits for them, and re-layouts  1.88 us

profile of v3, /device:TPU:6, one launch (start us, length us, event | category | flops | bytes accessed | tf_op | source)
XLA Modules:
  0.0 64.9 jit_solution(6504892631328188660)
XLA Ops:
  0.0 63.0 %shard_map.154 = bf16[128,2048]{1,0:T(8,128)(2,1)} custom-call(s32[4,8]{1,0:T(4,128)} %bitcast.2, s32[4,126]{1,0:T(4,128)} %bitcast.3, bf16[128,2048]{1,0:T(8,128)(2,1)} %rhs.1, bf16[64,2048]{1,0:T(8,128)(2,1)} %col.1, f32[8,4096]{1,0:T(8,128)} %leaf_up.1, f32[8,4096]{1,0:T(8,128)} %leaf_down.1, f32[7,4096]{1,0:T(8,128)} %local_up.1, f32[7,4096]{1,0:T(8,128)} %local_down.1, ...), custom_call_target="tpu_custom_call" | custom-call | tf_op jit(solution)/shard_map/pallas_call | solution.py:477
  63.1 1.9 %copy.18 = bf16[128,2048]{1,0:T(8,128)(2,1)} copy(bf16[128,2048]{1,0:T(8,128)(2,1)} %shard_map.154) | data formatting | bytes 1048576

commit v4 on v3

--- a/solution.py
+++ b/solution.py
@@ -231,7 +231,7 @@
         remote(send_b.at[g], recv_b.at[:, zc], 4, at_zc(g))
         return 0
 
-    lax.fori_loop(1, 3, step_first, 0)
+    lax.fori_loop(1, 4, step_first, 0)
     finish(roots.at[pl.ds(0, 3)], recv_sem.at[6])
     first_lanes = lax.broadcasted_iota(jnp.int32, (R, 2 * K), 1) < K
     r = [roots[h].astype(F32) for h in range(4)]
@@ -242,19 +242,18 @@
     for z in others(cz, 4):
         remote(mine, mine, 7, at_z(z))
 
-    lax.fori_loop(3, 5, step_first, 0)
+    lax.fori_loop(4, 7, step_first, 0)
     finish(tiles_hi.at[pl.ds(0, 3)], recv_sem.at[7])
     column = tiles_hi.at[mx * 4 + cy]
     for x in others(cx, 4):
         remote(column, column, 10, at_x(x))
 
-    lax.fori_loop(5, 7, step_first, 0)
+    lax.fori_loop(7, 8, step_first, 0)
     finish(tiles_hi.at[pl.ds(0, 3)], recv_sem.at[10])
     for x in others(cx, 4):
         column = tiles_hi.at[(x * 2 + cc) * 4 + cy]
         for y in others(cy, 4):
             remote(column, column, 14, at_y(y))
-    lax.fori_loop(7, 8, step_first, 0)
     place_a(mx)
     place_b(zc)
     recv_a[:, mx] = send_a[mx]

time: 65.1 us -> 71.4 us (1.097)
  Pallas kernels: 63 us -> 69.3 us
    pallas_call x1, Pallas kernels: 63 us -> 69.3 us  [body(): pl.pallas_call(kernel, out_shape=jax.ShapeDtypeStruct((R, width), BF), in...]
where the time goes in v4:
time: 71.4 us; the launch traced here: 71.2 us
  Pallas kernels  69.3 us (97%)
  local copies, waits for them, and re-layouts  1.88 us (3%)
    pallas_call x1, Pallas kernels, body(): pl.pallas_call(kernel, out_shape=jax.ShapeDtypeStruct((R, width), BF), in...  69.3 us
    unnamed x1, local copies, waits for them, and re-layouts  1.88 us

profile of v4, /device:TPU:6, one launch (start us, length us, event | category | flops | bytes accessed | tf_op | source)
XLA Modules:
  0.0 71.2 jit_solution(6798162506336574789)
XLA Ops:
  0.0 69.3 %shard_map.154 = bf16[128,2048]{1,0:T(8,128)(2,1)} custom-call(s32[4,8]{1,0:T(4,128)} %bitcast.2, s32[4,126]{1,0:T(4,128)} %bitcast.3, bf16[128,2048]{1,0:T(8,128)(2,1)} %rhs.1, bf16[64,2048]{1,0:T(8,128)(2,1)} %col.1, f32[8,4096]{1,0:T(8,128)} %leaf_up.1, f32[8,4096]{1,0:T(8,128)} %leaf_down.1, f32[7,4096]{1,0:T(8,128)} %local_up.1, f32[7,4096]{1,0:T(8,128)} %local_down.1, ...), custom_call_target="tpu_custom_call" | custom-call | tf_op jit(solution)/shard_map/pallas_call | solution.py:476
  69.3 1.9 %copy.18 = bf16[128,2048]{1,0:T(8,128)(2,1)} copy(bf16[128,2048]{1,0:T(8,128)(2,1)} %shard_map.154) | data formatting | bytes 1048576
